TPU v7x, 256 devices: a whole 4x4x8 slice. The times are simulated.
256 devices in a mesh: section: 2 (over z_lo), row: 16 (over x, y), col: 8 (over z_hi, core).
Axes of the slice: x: 4, y: 4, z: 8 (z_hi: 4, z_lo: 2; z = z_hi * 2 + z_lo), core: 2. Of those that a mesh axis runs over, the one named last changes fastest.
Arguments:
- section_hidden: bfloat16 [2, 1024, 28672], P('section', 'row', 'col'), may hold values from -6 to 6
- section_weight: bfloat16 [2, 28672, 8192], P('section', 'col', 'row'), may hold values from -0.046875 to 0.046875
- resid_in: bfloat16 [2, 1024, 8192], P('section', 'col', 'row'), may hold values from -40 to 40, as said below
- norm_gain: bfloat16 [8192], P('row'), may hold values from 0.25 to 1.75
Outputs:
- weight_grads: bfloat16 [2, 28672, 8192], P('section', 'col', 'row')
- section_out: bfloat16 [2, 1024, 28672], P('section', 'row', 'col')
Inputs may be any that keep to these rules, and one draw needn't show every extreme that they name: `resid_in`: entries of order one with scales that differ from token to token and grow along the features.
All inputs are finite; a program needn't handle non-finite values.
Results may differ from a plain program's by a relative error of at most 0.0052.
Values may be sent and summed in bfloat16 or wider, within the bound.
A program may use at most 128 MiB of HBM per device.

v0:
```python
import jax
import jax.numpy as jnp
from jax import lax
from jax.sharding import PartitionSpec as P

epsilon = 1e-05


def passed_along(value, axis, steps):
    count = lax.axis_size(axis)
    leading, last = (max(0, -steps), min(count, count - steps))
    return lax.ppermute(value, axis, [(source, source + steps) for source in range(leading, last)])


def local(section_hidden, section_weight, resid_in, norm_gain):
    weight = section_weight[0]
    gain_f = norm_gain.astype(jnp.float32)
    is_first = lax.axis_index("section") == 0
    left_full = lax.all_gather(section_hidden[0], "row", axis=0, tiled=True)
    model_width = weight.shape[1] * lax.axis_size("row")
    first_sum = lax.psum(jnp.dot(left_full, weight, preferred_element_type=jnp.float32), "col")
    resid_part = lax.all_gather(resid_in[0], "col", axis=0, tiled=True).astype(jnp.float32)
    forward = (resid_part + first_sum).astype(jnp.bfloat16)
    arrived = passed_along(forward, "section", 1).astype(jnp.float32)
    squares, cross_sum = lax.psum(
        (jnp.sum(arrived * arrived, axis=1), jnp.sum(first_sum * gain_f * arrived, axis=1)), "row"
    )
    inv_rms = lax.rsqrt(squares / model_width + epsilon)[:, None]
    normed = (arrived * inv_rms * gain_f).astype(jnp.bfloat16)
    back_tile = (
        resid_part
        + inv_rms * gain_f * first_sum
        - arrived * inv_rms**3 * (cross_sum / model_width)[:, None]
    ).astype(jnp.bfloat16)
    returned = passed_along(back_tile, "section", -1)
    local_right = jnp.where(is_first, returned, normed)
    second_sum = lax.psum_scatter(
        lax.dot_general(
            local_right, weight, (((1,), (1,)), ((), ())), preferred_element_type=jnp.float32
        ),
        "row",
        scatter_dimension=0,
        tiled=True,
    )
    weight_grad = lax.dot_general(
        left_full, local_right, (((0,), (0,)), ((), ())), preferred_element_type=jnp.float32
    ).astype(jnp.bfloat16)
    return (weight_grad[None], second_sum.astype(jnp.bfloat16)[None])


def solution(mesh):
    in_specs = (
        P("section", "row", "col"),
        P("section", "col", "row"),
        P("section", "col", "row"),
        P("row"),
    )
    out_specs = (P("section", "col", "row"), P("section", "row", "col"))
    return jax.shard_map(local, mesh=mesh, in_specs=in_specs, out_specs=out_specs, check_vma=False)
```

profile of v0, /device:TPU:1, one launch (start us, length us, event | category | flops | bytes accessed | tf_op | source)
XLA Modules:
  0.0 411.7 jit_solution(15961474103361066504)
XLA Ops:
  7.2 0.0 all-gather.7.cloned.1.call-start
  7.2 0.7 all-gather.7.cloned.1.call-update
  7.9 0.0 all-gather.5.cloned.1.call-start
  7.9 0.7 all-gather.5.cloned.1.call-update
  8.6 0.0 all-reduce.3.cloned.1.call-start
  8.7 76.8 %all-gather.7.cloned.1.call-done = bf16[1,1024,3584]{2,1,0:T(8,128)(2,1)} async-done(((bf16[1,64,3584]{2,1,0:T(8,128)(2,1)}), bf16[1,1024,3584]{2,1,0:T(8,128)(2,1)}) %all-gather.7.cloned.1.call-update) | async-done | bytes 7340048 | tf_op jit(solution)/shard_map/all_gather | solution.py:19
  85.5 9.4 %fusion.2 = f32[1024,512]{1,0:T(8,128)} fusion(bf16[1,1024,3584]{2,1,0:T(8,128)(2,1)} %all-gather.7.cloned.1.call-done, bf16[1,3584,512]{2,1,0:T(8,128)(2,1)} %param.5), kind=kOutput, calls=%fused_computation.2 | convolution fusion | flops 3758096384 | bytes 13107200 | tf_op jit(solution)/shard_map/dot_general | solution.py:21
  94.9 0.0 all-reduce.3.cloned.1.call-update
  94.9 0.0 copy-start.1
  94.9 0.0 reduce-scatter.2.cloned.1.call-start
  94.9 22.6 %all-gather.5.cloned.1.call-done = bf16[1,1024,512]{2,1,0:T(8,128)(2,1)} async-done(((bf16[1,128,512]{2,1,0:T(8,128)(2,1)}), bf16[1,1024,512]{2,1,0:T(8,128)(2,1)}) %all-gather.5.cloned.1.call-update) | async-done | bytes 1048592 | tf_op jit(solution)/shard_map/all_gather | solution.py:22
  117.5 84.7 %all-reduce.3.cloned.1.call-done = f32[1024,512]{1,0:T(8,128)} async-done(((f32[1024,512]{1,0:T(8,128)}), f32[1024,512]{1,0:T(8,128)}) %all-reduce.3.cloned.1.call-update) | async-done | bytes 2097168 | tf_op jit(solution)/shard_map/psum | solution.py:21
  202.2 0.0 copy-start
  202.2 2.4 fusion.13
  204.6 2.9 collective-permute-start
  207.5 0.0 copy-done.1
  207.5 21.1 %collective-permute-done = bf16[1024,512]{1,0:T(8,128)(2,1)S(1)} collective-permute-done((bf16[1024,512]{1,0:T(8,128)(2,1)S(1)}, bf16[1024,512]{1,0:T(8,128)(2,1)S(1)}, u32[]{:S(2)}, u32[]{:S(2)}) %collective-permute-start) | collective-permute-done | bytes 1048608 | tf_op jit(solution)/shard_map/ppermute | solution.py:12
  228.6 0.0 copy-done
  228.6 0.5 fusion.16
  229.1 33.3 %all-reduce = (f32[1024]{0:T(1024)S(1)}, f32[1024]{0:T(1024)S(1)}) all-reduce(f32[1024]{0:T(1024)S(1)} %get-tuple-element.5, f32[1024]{0:T(1024)S(1)} %get-tuple-element.4), channel_id=1, replica_groups=mesh['section'=2,'row'=16,'col'=8] {'row'}, use_global_device_ids=true, to_apply=%region_4.0 | all-reduce | flops 2048 | bytes 16384 | tf_op jit(solution)/shard_map/psum | solution.py:25
  262.4 2.8 fusion.15
  265.2 1.3 collective-permute-start.1
  266.5 15.9 %collective-permute-done.1 = bf16[1024,512]{1,0:T(8,128)(2,1)S(1)} collective-permute-done((bf16[1024,512]{1,0:T(8,128)(2,1)}, bf16[1024,512]{1,0:T(8,128)(2,1)S(1)}, u32[]{:S(2)}, u32[]{:S(2)}) %collective-permute-start.1) | collective-permute-done | bytes 1048608 | tf_op jit(solution)/shard_map/ppermute | solution.py:12
  282.5 9.5 %fusion.10 = f32[1024,3584]{1,0:T(8,128)} fusion(bf16[1,3584,512]{2,1,0:T(8,128)(2,1)} %param.5, bf16[1024,512]{1,0:T(8,128)(2,1)S(1)} %collective-permute-done.1, bf16[1024,512]{1,0:T(8,128)(2,1)S(1)} %collective-permute-done, f32[512]{0:T(512)S(1)} %convert_element_type.30, f32[1024]{0:T(1024)S(1)} %get-tuple-element.8, pred[]{:T(512)S(6)} %eq.3), kind=kOutput, calls=%fused_computation.6 | convolution fusion | flops 3760717824 | bytes 20453376 | tf_op jit(solution)/shard_map/dot_general | solution.py:38
  292.0 0.0 reduce-scatter.2.cloned.1.call-update
  292.0 8.8 %fusion.7 = bf16[1,3584,512]{1,2,0:T(8,128)(2,1)} fusion(bf16[1,1024,3584]{2,1,0:T(8,128)(2,1)} %all-gather.7.cloned.1.call-done, bf16[1024,512]{1,0:T(8,128)(2,1)S(1)} %collective-permute-done.1, bf16[1024,512]{1,0:T(8,128)(2,1)S(1)} %collective-permute-done, f32[512]{0:T(512)S(1)} %convert_element_type.30, f32[1024]{0:T(1024)S(1)} %get-tuple-element.8, ...), kind=kOutput, calls=%fused_computation.5 | convolution fusion | flops 3762552832 | bytes 13113345 | tf_op jit(solution)/shard_map/dot_general | solution.py:45
  300.8 5.9 %copy.6 = bf16[1,3584,512]{2,1,0:T(8,128)(2,1)} copy(bf16[1,3584,512]{1,2,0:T(8,128)(2,1)} %fusion.7) | data formatting | bytes 7340032
  306.7 96.4 %reduce-scatter.2.cloned.1.call-done = f32[64,3584]{1,0:T(8,128)} async-done(((f32[1024,3584]{1,0:T(8,128)}), f32[64,3584]{1,0:T(8,128)}) %reduce-scatter.2.cloned.1.call-update) | async-done | bytes 917520 | tf_op jit(solution)/shard_map/reduce_scatter | solution.py:37
  403.1 2.0 convert_bitcast_fusion
  (2 shorter events, 0.0 us)
Async XLA Ops:
  7.2 78.3 %all-gather.7.cloned.1.call-start = ((), (), s32[]{:S(2)}) async-start(), calls=%async_computation.4 | async-start | bytes 7798784 | tf_op jit(solution)/shard_map/all_gather | solution.py:19
  7.9 109.6 %all-gather.5.cloned.1.call-start = ((), (), s32[]{:S(2)}) async-start(), calls=%async_computation.3 | async-start | bytes 1179648 | tf_op jit(solution)/shard_map/all_gather | solution.py:22
  8.6 193.6 %all-reduce.3.cloned.1.call-start = ((), (), s32[]{:S(2)}) async-start(), calls=%async_computation.1 | async-start | bytes 4194304 | tf_op jit(solution)/shard_map/psum | solution.py:21
  94.9 112.6 %copy-start.1 = (bf16[512]{0:T(512)(128)(2,1)S(1)}, bf16[512]{0:T(512)(128)(2,1)}, u32[]{:S(2)}) copy-start(bf16[512]{0:T(512)(128)(2,1)} %param.7) | copy-start | bytes 3076
  94.9 308.2 %reduce-scatter.2.cloned.1.call-start = ((), (), s32[]{:S(2)}) async-start(), calls=%async_computation.2 | async-start | bytes 15597568 | tf_op jit(solution)/shard_map/reduce_scatter | solution.py:37
  202.2 26.4 %copy-start = (f32[1024,512]{1,0:T(8,128)S(1)}, f32[1024,512]{1,0:T(8,128)}, u32[]{:S(2)}) copy-start(f32[1024,512]{1,0:T(8,128)} %all-reduce.3.cloned.1.call-done) | copy-start | bytes 6291460
  204.6 24.0 %collective-permute-start = (bf16[1024,512]{1,0:T(8,128)(2,1)S(1)}, bf16[1024,512]{1,0:T(8,128)(2,1)S(1)}, u32[]{:S(2)}, u32[]{:S(2)}) collective-permute-start(bf16[1024,512]{1,0:T(8,128)(2,1)S(1)} %fusion.13), channel_id=1, source_target_pairs={{0,128},{1,129},{2,130},{3,131},{4,132},{5,133},{6,134},{7,135},{8... | collective-permute-start | bytes 3145736 | tf_op jit(solution)/shard_map/ppermute | solution.py:12
  265.2 17.2 %collective-permute-start.1 = (bf16[1024,512]{1,0:T(8,128)(2,1)}, bf16[1024,512]{1,0:T(8,128)(2,1)S(1)}, u32[]{:S(2)}, u32[]{:S(2)}) collective-permute-start(bf16[1024,512]{1,0:T(8,128)(2,1)} %fusion.15), channel_id=1, source_target_pairs={{128,0},{129,1},{130,2},{131,3},{132,4},{133,5},{134,6},{135,7},{1... | collective-permute-start | bytes 3145736 | tf_op jit(solution)/shard_map/ppermute | solution.py:12
Sparse Core Ops, SparseCore 0:
  10.5 74.9 all-gather.6
  87.3 30.1 all-gather.4
  120.8 81.3 all-reduce.2
  292.1 110.9 reduce-scatter.1
where the time goes:
time: 412 us
  waiting for transfers between devices  319 us (77%)
  blocking collectives  33.3 us (8%)
  matrix products  27.7 us (7%)
  between operations  13.8 us (3%)
  other arithmetic  7.69 us (2%)
  local copies, waits for them, and re-layouts  5.93 us (1%)
  starting transfers between devices  4.35 us (1%)
    reduce_scatter x1, waiting for transfers between devices, local(): lax.psum_scatter(lax.dot_general(local_right, weight, (((1,), (1,)), ((),...  96.4 us
    psum x1, waiting for transfers between devices, local(): lax.psum(jnp.dot(left_full, weight, preferred_element_type=jnp.float32),...  84.7 us
    all_gather x1, waiting for transfers between devices, local(): left_full = lax.all_gather(section_hidden[0], 'row', axis=0, tiled=True)  76.8 us
    ppermute x2, waiting for transfers between devices, passed_along(): lax.ppermute(value, axis, [(source, source + steps) for source in range(l...  37 us
    psum x1, blocking collectives, local(): lax.psum((jnp.sum(arrived * arrived, axis=1), jnp.sum(first_sum * gain_f...  33.3 us
    all_gather x1, waiting for transfers between devices, local(): lax.all_gather(resid_in[0], 'col', axis=0, tiled=True).astype(jnp.float32)  22.6 us
    dot_general x1, matrix products, local(): lax.dot_general(local_right, weight, (((1,), (1,)), ((), ())), preferred_...  9.5 us
    dot_general x1, matrix products, local(): jnp.dot(left_full, weight, preferred_element_type=jnp.float32)  9.38 us
  transfers between devices with their start and end apart: 6, of which 6 were waited for; matrix products, arithmetic and copies ran while one was open for 6% of the time, Pallas kernels for 0%

commit v1 on v0

v1 whole, which is shorter than its diff:
```python
import functools

import jax
import jax.numpy as jnp
from jax import lax
from jax.experimental import pallas as pl
from jax.experimental.pallas import tpu as pltpu
from jax.sharding import PartitionSpec as P

EPS = 1e-05
MESH = pl.DeviceIdType.MESH
F32 = jnp.float32
BF16 = jnp.bfloat16
K = 2
Q = 4
ALL = slice(None)


def mask_of(pos, mask):
    if mask == 1:
        return pos + 1 - 2 * lax.rem(pos, 2)
    if mask == 3:
        return 3 - pos
    return lax.rem(pos + 2, 4)


def gray(pos):
    high = lax.div(pos, 2)
    low = lax.rem(pos, 2)
    return high, high + low - 2 * high * low


def kernel(model_width, hidden, weight, resid, gain, grads, out, *scratch):
    (w, h, z, rc, rz1, rz2, own_resid, far_resid, swap_s, swap_r, ps_s, ps_x, ps_t, ps_y, x_, p2, r0, r1, r2, r3,
     outv, gv, l_w, l_h, l_r, l_o, l_g,
     ag_s, ag_r, rs_s, rs_r, zc_s, zc_r, z1_s, z1_r, z2_s, z2_r, q_s, q_r, sw_s, sw_r, px_s, px_r, py_s, py_r,
     x1_s, x1_r, x2_s, x2_r, xc_s, xc_r) = scratch
    rest = [r0, r1, r2, r3]
    tokens = hidden.shape[1] // K
    width = hidden.shape[2] // Q
    half = weight.shape[2] // 2
    sec = lax.axis_index("section")
    row = lax.axis_index("row")
    col = lax.axis_index("col")
    px, py = lax.div(row, 4), lax.rem(row, 4)
    zh, core = lax.div(col, 2), lax.rem(col, 2)
    gx1, gx0 = gray(px)
    gy1, gy0 = gray(py)
    gz1, gz0 = gray(zh)
    bits = [gx1, gx0, gy1, gy0]
    flips = [
        {"row": mask_of(px, 3) * 4 + py},
        {"row": mask_of(px, 1) * 4 + py},
        {"row": px * 4 + mask_of(py, 3)},
        {"row": px * 4 + mask_of(py, 1)},
    ]
    x_peers = [{"row": mask_of(px, m) * 4 + py} for m in (1, 2, 3)]
    y_peers = [{"row": px * 4 + mask_of(py, m)} for m in (1, 2, 3)]
    core_peer = {"col": zh * 2 + 1 - core}
    z_low = {"col": mask_of(zh, 1) * 2 + core}
    z_high = {"col": mask_of(zh, 3) * 2 + core}
    sec_peer = {"section": 1 - sec}

    barrier = pltpu.get_barrier_semaphore()
    partners = x_peers + y_peers + [core_peer, z_low, z_high, sec_peer]
    for peer in partners:
        pl.semaphore_signal(barrier, inc=1, device_id=peer, device_id_type=MESH)

    loads = []

    def load(src, dst, sem):
        copy = pltpu.make_async_copy(src, dst, sem)
        copy.start()
        return copy

    def own_block(k, q):
        return hidden.at[0, pl.ds(k * tokens, tokens), pl.ds(q * width, width)]

    h_loads = [[load(own_block(k, q), h.at[q, k, gx1, gx0, gy1, gy0], l_h.at[k, q]) for q in range(Q)] for k in range(K)]
    g_load = load(gain, gv, l_g)
    w_load = load(weight.at[0], w, l_w)
    start0 = pl.multiple_of(64 * core, 64)
    start1 = pl.multiple_of(64 * (1 - core), 64)
    r_loads = [
        [load(resid.at[0, pl.ds(start + k * tokens, tokens), :], own_resid.at[k, b], l_r.at[k, b]) for b, start in enumerate((start0, start1))]
        for k in range(K)
    ]

    pl.semaphore_wait(barrier, len(partners))

    sends = []

    def send(src, dst, ssem, rsem, peer):
        copy = pltpu.make_async_remote_copy(src, dst, ssem, rsem, device_id=peer, device_id_type=MESH)
        copy.start()
        sends.append(copy)
        return copy

    ag = {}

    def ag_index(q, i):
        free = {(q + n) % 4 for n in range(i)}
        return tuple(ALL if d in free else bits[d] for d in range(4))

    def ag_send(k, i):
        for q in range(Q):
            if i > 0:
                ag[k, q, i - 1].wait_recv()
            if i == 1:
                h_loads[k][q].wait()
            index = (q, k) + ag_index(q, i)
            src = own_block(k, q) if i == 0 else h.at[index]
            ag[k, q, i] = send(src, h.at[index], ag_s.at[k, q, i], ag_r.at[k, q, i], flips[(q + i) % 4])

    def ag_done(k):
        for q in range(Q):
            ag[k, q, 3].wait_recv()

    zc, z1, z2, sw, pxs, pys, x1, x2, xc, rs = {}, {}, {}, {}, {}, {}, {}, {}, {}, {}

    def first(k):
        if k == 0:
            w_load.wait()

        def tile(a):
            acc = None
            for q in range(Q):
                lhs = h[q, k, a].reshape(8 * tokens, width)
                term = jnp.dot(lhs, w[pl.ds(q * width, width), :], preferred_element_type=F32)
                acc = term if acc is None else acc + term
            for s in range(2):
                z[k, s, a] = acc[:, s * half : (s + 1) * half].reshape(2, 2, 2 * tokens, half)

        pl.loop(0, 2)(tile)
        zc[k] = send(z.at[k, :, :, :, 1 - core], rc.at[k], zc_s.at[k], zc_r.at[k], core_peer)

    def after_core(k):
        zc[k].wait_recv()
        z[k, :, :, :, core] = z[k, :, :, :, core] + rc[k]
        z1[k] = [
            send(z.at[k, 0, :, 1 - gz0, core], rz1.at[k, 0], z1_s.at[k, 0], z1_r.at[k, 0], z_low),
            send(z.at[k, 1, 1 - gz1, :, core], rz1.at[k, 1], z1_s.at[k, 1], z1_r.at[k, 1], z_high),
        ]

    def after_z1(k):
        z1[k][0].wait_recv()
        z[k, 0, :, gz0, core] = z[k, 0, :, gz0, core] + rz1[k, 0]
        first_half = send(z.at[k, 0, 1 - gz1, gz0, core], rz2.at[k, 0], z2_s.at[k, 0], z2_r.at[k, 0], z_high)
        z1[k][1].wait_recv()
        z[k, 1, gz1, :, core] = z[k, 1, gz1, :, core] + rz1[k, 1]
        z2[k] = [first_half, send(z.at[k, 1, gz1, 1 - gz0, core], rz2.at[k, 1], z2_s.at[k, 1], z2_r.at[k, 1], z_low)]

    def after_z2(k):
        for b in range(2):
            r_loads[k][b].wait()
        for s in range(2):
            z2[k][s].wait_recv()
            total = z[k, s, gz1, gz0, core] + rz2[k, s]
            res = own_resid[k, :, :, s * half : (s + 1) * half].reshape(2 * tokens, half).astype(F32)
            layer = (res + total).astype(BF16).astype(F32)
            swap_s[k, :, s * half : (s + 1) * half] = jnp.where(sec == 0, layer, total)
        sw[k] = send(swap_s.at[k], swap_r.at[k], sw_s.at[k], sw_r.at[k], sec_peer)

    def after_swap(k):
        if k == 0:
            g_load.wait()
        sw[k].wait_recv()
        mine, theirs = swap_s[k], swap_r[k]
        layer = jnp.where(sec == 0, mine, theirs)
        total = jnp.where(sec == 0, theirs, mine)
        gain_f = gv[...].astype(F32)
        squares = jnp.sum(layer * layer, axis=1, keepdims=True)
        cross = jnp.sum(total * gain_f * layer, axis=1, keepdims=True)
        lane = lax.broadcasted_iota(jnp.int32, (2 * tokens, 128), 1)
        ps_s[k] = jnp.where(lane < 64, squares, cross)
        pxs[k] = [send(ps_s.at[k], ps_x.at[k, n], px_s.at[k, n], px_r.at[k, n], x_peers[n]) for n in range(3)]

    def after_px(k):
        for copy in pxs[k]:
            copy.wait_recv()
        ps_t[k] = (ps_s[k] + ps_x[k, 0]) + (ps_x[k, 1] + ps_x[k, 2])
        pys[k] = [send(ps_t.at[k], ps_y.at[k, n], py_s.at[k, n], py_r.at[k, n], y_peers[n]) for n in range(3)]

    def after_py(k):
        for copy in pys[k]:
            copy.wait_recv()
        if k == 0:
            for copy in far:
                copy.wait_recv()
        sums = (ps_t[k] + ps_y[k, 0]) + (ps_y[k, 1] + ps_y[k, 2])
        inv_rms = lax.rsqrt(sums[:, 0:1] / model_width + EPS)
        cross = sums[:, 64:65] / model_width
        scale = inv_rms * inv_rms * inv_rms * cross
        mine, theirs = swap_s[k], swap_r[k]
        layer = jnp.where(sec == 0, mine, theirs)
        total = jnp.where(sec == 0, theirs, mine)
        gain_f = gv[...].astype(F32)
        other = far_resid[k].reshape(2 * tokens, 2 * half).astype(F32)
        normed = layer * inv_rms * gain_f
        grad_in = other + inv_rms * gain_f * total - layer * scale
        value = jnp.where(sec == 0, grad_in, normed).astype(BF16)
        x_[k, 0, gz1, gz0, core] = value[:, :half]
        x_[k, 1, gz1, gz0, core] = value[:, half:]
        for s, peer in enumerate((z_low, z_high)):
            part = x_.at[k, s, gz1, gz0, core]
            x1[k, s] = send(part, part, x1_s.at[k, s], x1_r.at[k, s], peer)

    def after_x1(k):
        parts = (x_.at[k, 0, gz1, :, core], x_.at[k, 1, :, gz0, core])
        for s, peer in enumerate((z_high, z_low)):
            x1[k, s].wait_recv()
            x2[k, s] = send(parts[s], parts[s], x2_s.at[k, s], x2_r.at[k, s], peer)

    def after_x2(k):
        for s in range(2):
            x2[k, s].wait_recv()
        part = x_.at[k, :, :, :, core]
        xc[k] = send(part, part, xc_s.at[k], xc_r.at[k], core_peer)

    def rs_index(q, i, value):
        done = {(q + 3 - n) % 4 for n in range(i)}
        now = (q + 3 - i) % 4
        return tuple(value if d == now else bits[d] if d in done else ALL for d in range(4)), now

    def rs_send(k, q, i):
        now = (q + 3 - i) % 4
        index, _ = rs_index(q, i, 1 - bits[now])
        rs[k, q, i] = send(p2.at[(k, q) + index], rest[i].at[k, q], rs_s.at[k, q, i], rs_r.at[k, q, i], flips[now])

    def second(k):
        xc[k].wait_recv()
        for q in range(Q):

            def tile(a, q=q):
                acc = None
                for s in range(2):
                    lhs = x_[k, s, a].reshape(8 * tokens, half)
                    rhs = w[pl.ds(q * width, width), s * half : (s + 1) * half]
                    term = lax.dot_general(lhs, rhs, (((1,), (1,)), ((), ())), preferred_element_type=F32)
                    acc = term if acc is None else acc + term
                p2[k, q, a] = acc.astype(BF16).reshape(2, 2, 2, tokens, width)

            pl.loop(0, 2)(tile)
            rs_send(k, q, 0)

    def rs_step(k, i):
        for q in range(Q):
            now = (q + 3 - i) % 4
            rs[k, q, i].wait_recv()
            index, _ = rs_index(q, i, bits[now])
            index = (k, q) + index
            total = p2[index].astype(F32) + rest[i][k, q].astype(F32)
            if i < 3:
                p2[index] = total.astype(BF16)
                rs_send(k, q, i + 1)
            else:
                outv[pl.ds(k * tokens, tokens), pl.ds(q * width, width)] = total.astype(BF16)

    def weight_grads(q):
        lhs = h[q].reshape(K * 16 * tokens, width)
        for s in range(2):
            rhs = x_[:, s].reshape(K * 16 * tokens, half)
            value = lax.dot_general(lhs, rhs, (((0,), (0,)), ((), ())), preferred_element_type=F32)
            grads[0, pl.ds(q * width, width), s * half : (s + 1) * half] = value.astype(BF16)

    for i in range(4):
        ag_send(0, i)
    far = [
        send(resid.at[0, pl.ds(start + k * tokens, tokens), :], far_resid.at[k, b], q_s.at[k, b], q_r.at[k, b], sec_peer)
        for k in range(K)
        for b, start in enumerate((start0, start1))
    ]
    ag_send(1, 0)
    ag_done(0)
    first(0)
    ag_send(1, 1)
    ag_send(1, 2)
    after_core(0)
    ag_send(1, 3)
    after_z1(0)
    after_z2(0)
    after_swap(0)
    after_px(0)
    after_py(0)
    after_x1(0)
    ag_done(1)
    first(1)
    after_x2(0)
    after_core(1)
    second(0)
    after_z1(1)
    after_z2(1)
    after_swap(1)
    after_px(1)
    after_py(1)
    rs_step(0, 0)
    after_x1(1)
    rs_step(0, 1)
    after_x2(1)
    rs_step(0, 2)
    second(1)
    rs_step(0, 3)
    weight_grads(0)
    weight_grads(1)
    rs_step(1, 0)
    weight_grads(2)
    rs_step(1, 1)
    weight_grads(3)
    rs_step(1, 2)
    rs_step(1, 3)
    final = load(outv, out.at[0], l_o)
    for copy in sends:
        copy.wait_send()
    final.wait()


def local(section_hidden, section_weight, resid_in, norm_gain):
    _, rows, units = section_hidden.shape
    _, _, features = section_weight.shape
    tokens, width, half = rows // K, units // Q, features // 2
    model_width = features * lax.axis_size("row")
    vmem, dma = pltpu.VMEM, pltpu.SemaphoreType.DMA
    cube = (2, 2, 2, 2)
    scratch = [
        vmem((units, features), BF16),
        vmem((Q, K) + cube + (tokens, width), BF16),
        vmem((K, 2, 2, 2, 2, 2 * tokens, half), F32),
        vmem((K, 2, 2, 2, 2 * tokens, half), F32),
        vmem((K, 2, 2, 2 * tokens, half), F32),
        vmem((K, 2, 2 * tokens, half), F32),
        vmem((K, 2, tokens, features), BF16),
        vmem((K, 2, tokens, features), BF16),
        vmem((K, 2 * tokens, features), F32),
        vmem((K, 2 * tokens, features), F32),
        vmem((K, 2 * tokens, 128), F32),
        vmem((K, 3, 2 * tokens, 128), F32),
        vmem((K, 2 * tokens, 128), F32),
        vmem((K, 3, 2 * tokens, 128), F32),
        vmem((K, 2, 2, 2, 2, 2 * tokens, half), BF16),
        vmem((K, Q) + cube + (tokens, width), BF16),
        vmem((K, Q, 2, 2, 2, tokens, width), BF16),
        vmem((K, Q, 2, 2, tokens, width), BF16),
        vmem((K, Q, 2, tokens, width), BF16),
        vmem((K, Q, tokens, width), BF16),
        vmem((rows, units), BF16),
        vmem((1, features), BF16),
        dma, dma((K, Q)), dma((K, 2)), dma, dma,
    ]
    for shape in ((K, Q, 4), (K, Q, 4), (K,), (K, 2), (K, 2), (K, 2), (K,), (K, 3), (K, 3), (K, 2), (K, 2), (K,)):
        scratch += [dma(shape), dma(shape)]
    hbm = pl.BlockSpec(memory_space=pl.ANY)
    flops = 3 * 2 * rows * 16 * units * features
    return pl.pallas_call(
        functools.partial(kernel, float(model_width)),
        out_shape=(
            jax.ShapeDtypeStruct((1, units, features), BF16),
            jax.ShapeDtypeStruct((1, rows, units), BF16),
        ),
        in_specs=[hbm] * 4,
        out_specs=(pl.BlockSpec(memory_space=pltpu.VMEM), hbm),
        scratch_shapes=scratch,
        compiler_params=pltpu.CompilerParams(collective_id=0, has_side_effects=True, vmem_limit_bytes=60 * 2**20),
        cost_estimate=pl.CostEstimate(flops=flops, bytes_accessed=10 * units * features, transcendentals=0),
    )(section_hidden, section_weight, resid_in, norm_gain.reshape(1, features))


def solution(mesh):
    in_specs = (
        P("section", "row", "col"),
        P("section", "col", "row"),
        P("section", "col", "row"),
        P("row"),
    )
    out_specs = (P("section", "col", "row"), P("section", "row", "col"))
    return jax.shard_map(local, mesh=mesh, in_specs=in_specs, out_specs=out_specs, check_vma=False)
```

time: 412 us -> 154 us (0.37)
  waiting for transfers between devices: 319 us -> 0 us
  Pallas kernels: 0 us -> 144 us
  blocking collectives: 33.3 us -> 0 us
  matrix products: 27.7 us -> 0 us
  between operations: 13.8 us -> 0.65 us
  other arithmetic: 7.69 us -> 0 us
  starting transfers between devices: 4.35 us -> 0 us
    pallas_call x0 -> x1, Pallas kernels: none -> 144 us  [local(): pl.pallas_call(functools.partial(kernel, float(model_width)), out_shape=(...]
    all_gather x2 -> x0, waiting for transfers between devices: 99.4 us -> none  [the longest x1 76.8 us: local(): left_full = lax.all_gather(section_hidden[0], 'row', axis=0, tiled=True)]
    reduce_scatter x1 -> x0, waiting for transfers between devices: 96.4 us -> none  [local(): lax.psum_scatter(lax.dot_general(local_right, weight, (((1,), (1,)), ((),...]
    psum x1 -> x0, waiting for transfers between devices: 84.7 us -> none  [local(): lax.psum(jnp.dot(left_full, weight, preferred_element_type=jnp.float32),...]
    ppermute x2 -> x0, waiting for transfers between devices: 37 us -> none  [passed_along(): lax.ppermute(value, axis, [(source, source + steps) for source in range(l...]
    psum x1 -> x0, blocking collectives: 33.3 us -> none  [local(): lax.psum((jnp.sum(arrived * arrived, axis=1), jnp.sum(first_sum * gain_f...]
    dot_general x3 -> x0, matrix products: 27.7 us -> none  [the longest x1 9.5 us: local(): lax.dot_general(local_right, weight, (((1,), (1,)), ((), ())), preferred_...]
    convert_element_type x3 -> x0, other arithmetic: 5.2 us -> none  [the longest x1 2.85 us: local(): back_tile = (resid_part + inv_rms * gain_f * first_sum - arrived * inv_rm...]
  transfers between devices with their start and end apart: 6 -> 0, of which waited for: 6 -> 0; matrix products, arithmetic and copies ran while one was open for 6% -> 0% of each run, Pallas kernels for 0% -> 0%
where the time goes in v1:
time: 154 us; the launch traced here: 151 us
  Pallas kernels  144 us (94%)
  local copies, waits for them, and re-layouts  6.2 us (4%)
    pallas_call x1, Pallas kernels, local(): pl.pallas_call(functools.partial(kernel, float(model_width)), out_shape=(...  144 us
    unnamed x4, local copies, waits for them, and re-layouts  4.94 us

profile of v1, /device:TPU:1, one launch (start us, length us, event | category | flops | bytes accessed | tf_op | source)
XLA Modules:
  0.0 151.3 jit_solution(15446889258166820403)
XLA Ops:
  0.6 1.3 reshape.7.gain
  1.9 144.4 %shard_map.59 = (bf16[1,3584,512]{2,1,0:T(8,128)(2,1)}, bf16[1,64,3584]{2,1,0:T(8,128)(2,1)}) custom-call(bf16[1,64,3584]{2,1,0:T(8,128)(2,1)} %hidden.1, bf16[1,3584,512]{2,1,0:T(8,128)(2,1)} %weight.1, bf16[1,128,512]{2,1,0:T(8,128)(2,1)} %resid.1, bf16[1,512]{1,0:T(2,128)(2,1)} %reshape.7.gain), custom_call_target="tpu_custom_call" | custom-call | flops 11274289152 | bytes 18350080 | tf_op jit(solution)/shard_map/pallas_call | solution.py:353
  146.3 0.0 copy-start
  146.4 4.2 %copy.8 = bf16[1,3584,512]{2,1,0:T(8,128)(2,1)} copy(bf16[1,3584,512]{2,1,0:T(8,128)(2,1)} %get-tuple-element.4) | data formatting | bytes 7340032
  150.5 0.0 copy-done
  150.5 0.8 copy.9
Async XLA Ops:
  146.3 4.2 %copy-start = (bf16[1,64,3584]{2,1,0:T(8,128)(2,1)S(1)}, bf16[1,64,3584]{2,1,0:T(8,128)(2,1)}, u32[]{:S(2)}) copy-start(bf16[1,64,3584]{2,1,0:T(8,128)(2,1)} %get-tuple-element.5) | copy-start | bytes 1376260

commit v2 on v1

--- a/solution.py
+++ b/solution.py
@@ -11,12 +11,17 @@
 MESH = pl.DeviceIdType.MESH
 F32 = jnp.float32
 BF16 = jnp.bfloat16
-K = 2
+K = 4
 Q = 4
 ALL = slice(None)
 
+ORDER = (0, 1, 2, 3, 0, 2, 1, 3, 0, 1, 3, 0, 2, 1, 0, 2, 3, 0, 1, 0, 1, 2, 2, 0, 3, 1, 3, 0, 1, 2, 0, 3, 1, 2, 0, 3, 1, 2, 0, 3, 1, 0, 2, 3, 1, 2, 1, 3, 2, 0, 2, 3, 3, 1, 2, 3, 1, 2, 0, 3, 2, 0, 1, 3, 0, 2, 1, 3)
+FAR_AT = 10
+
 
 def mask_of(pos, mask):
+    if mask == 0:
+        return pos
     if mask == 1:
         return pos + 1 - 2 * lax.rem(pos, 2)
     if mask == 3:
@@ -31,11 +36,12 @@
 
 
 def kernel(model_width, hidden, weight, resid, gain, grads, out, *scratch):
-    (w, h, z, rc, rz1, rz2, own_resid, far_resid, swap_s, swap_r, ps_s, ps_x, ps_t, ps_y, x_, p2, r0, r1, r2, r3,
+    (w, h, z, rc, rz1, rz2, own_resid, far_resid, swap_s, swap_r, ps_s, ps_x, x_, own, t0, t1, t2, t3, r0, r1, r2, r3,
      outv, gv, l_w, l_h, l_r, l_o, l_g,
-     ag_s, ag_r, rs_s, rs_r, zc_s, zc_r, z1_s, z1_r, z2_s, z2_r, q_s, q_r, sw_s, sw_r, px_s, px_r, py_s, py_r,
+     ag_s, ag_r, rs_s, rs_r, zc_s, zc_r, z1_s, z1_r, z2_s, z2_r, q_s, q_r, sw_s, sw_r, px_s, px_r,
      x1_s, x1_r, x2_s, x2_r, xc_s, xc_r) = scratch
     rest = [r0, r1, r2, r3]
+    away = [t0, t1, t2, t3]
     tokens = hidden.shape[1] // K
     width = hidden.shape[2] // Q
     half = weight.shape[2] // 2
@@ -54,15 +60,14 @@
         {"row": px * 4 + mask_of(py, 3)},
         {"row": px * 4 + mask_of(py, 1)},
     ]
-    x_peers = [{"row": mask_of(px, m) * 4 + py} for m in (1, 2, 3)]
-    y_peers = [{"row": px * 4 + mask_of(py, m)} for m in (1, 2, 3)]
+    row_peers = [{"row": mask_of(px, m // 4) * 4 + mask_of(py, m % 4)} for m in range(1, 16)]
     core_peer = {"col": zh * 2 + 1 - core}
     z_low = {"col": mask_of(zh, 1) * 2 + core}
     z_high = {"col": mask_of(zh, 3) * 2 + core}
     sec_peer = {"section": 1 - sec}
 
     barrier = pltpu.get_barrier_semaphore()
-    partners = x_peers + y_peers + [core_peer, z_low, z_high, sec_peer]
+    partners = row_peers + [core_peer, z_low, z_high, sec_peer]
     for peer in partners:
         pl.semaphore_signal(barrier, inc=1, device_id=peer, device_id_type=MESH)
 
@@ -88,6 +93,10 @@
 
     pl.semaphore_wait(barrier, len(partners))
 
+    lane = lax.broadcasted_iota(jnp.int32, (2 * tokens, 128), 1)
+    token = lax.broadcasted_iota(jnp.int32, (2 * tokens, 128), 0)
+    at_square, at_cross = lane == token, lane == token + 2 * tokens
+
     sends = []
 
     def send(src, dst, ssem, rsem, peer):
@@ -116,22 +125,19 @@
         for q in range(Q):
             ag[k, q, 3].wait_recv()
 
-    zc, z1, z2, sw, pxs, pys, x1, x2, xc, rs = {}, {}, {}, {}, {}, {}, {}, {}, {}, {}
+    zc, z1, z2, sw, pxs, x1, x2, xc, rs = {}, {}, {}, {}, {}, {}, {}, {}, {}
 
     def first(k):
         if k == 0:
             w_load.wait()
 
-        def tile(a):
-            acc = None
-            for q in range(Q):
-                lhs = h[q, k, a].reshape(8 * tokens, width)
-                term = jnp.dot(lhs, w[pl.ds(q * width, width), :], preferred_element_type=F32)
-                acc = term if acc is None else acc + term
-            for s in range(2):
-                z[k, s, a] = acc[:, s * half : (s + 1) * half].reshape(2, 2, 2 * tokens, half)
-
-        pl.loop(0, 2)(tile)
+        acc = None
+        for q in range(Q):
+            lhs = h[q, k].reshape(16 * tokens, width)
+            term = jnp.dot(lhs, w[pl.ds(q * width, width), :], preferred_element_type=F32)
+            acc = term if acc is None else acc + term
+        for s in range(2):
+            z[k, s] = acc[:, s * half : (s + 1) * half].reshape(2, 2, 2, 2 * tokens, half)
         zc[k] = send(z.at[k, :, :, :, 1 - core], rc.at[k], zc_s.at[k], zc_r.at[k], core_peer)
 
     def after_core(k):
@@ -171,25 +177,20 @@
         gain_f = gv[...].astype(F32)
         squares = jnp.sum(layer * layer, axis=1, keepdims=True)
         cross = jnp.sum(total * gain_f * layer, axis=1, keepdims=True)
-        lane = lax.broadcasted_iota(jnp.int32, (2 * tokens, 128), 1)
-        ps_s[k] = jnp.where(lane < 64, squares, cross)
-        pxs[k] = [send(ps_s.at[k], ps_x.at[k, n], px_s.at[k, n], px_r.at[k, n], x_peers[n]) for n in range(3)]
-
-    def after_px(k):
+        line = jnp.where(at_square, squares, 0.0) + jnp.where(at_cross, cross, 0.0)
+        ps_s[k] = jnp.sum(line, axis=0, keepdims=True)
+        pxs[k] = [send(ps_s.at[k], ps_x.at[k, n], px_s.at[k, n], px_r.at[k, n], row_peers[n]) for n in range(15)]
+
+    def after_sums(k):
         for copy in pxs[k]:
-            copy.wait_recv()
-        ps_t[k] = (ps_s[k] + ps_x[k, 0]) + (ps_x[k, 1] + ps_x[k, 2])
-        pys[k] = [send(ps_t.at[k], ps_y.at[k, n], py_s.at[k, n], py_r.at[k, n], y_peers[n]) for n in range(3)]
-
-    def after_py(k):
-        for copy in pys[k]:
             copy.wait_recv()
         if k == 0:
             for copy in far:
                 copy.wait_recv()
-        sums = (ps_t[k] + ps_y[k, 0]) + (ps_y[k, 1] + ps_y[k, 2])
-        inv_rms = lax.rsqrt(sums[:, 0:1] / model_width + EPS)
-        cross = sums[:, 64:65] / model_width
+        line = ps_s[k] + jnp.sum(ps_x[k], axis=0)
+        squares = jnp.sum(jnp.where(at_square, line, 0.0), axis=1, keepdims=True)
+        cross = jnp.sum(jnp.where(at_cross, line, 0.0), axis=1, keepdims=True) / model_width
+        inv_rms = lax.rsqrt(squares / model_width + EPS)
         scale = inv_rms * inv_rms * inv_rms * cross
         mine, theirs = swap_s[k], swap_r[k]
         layer = jnp.where(sec == 0, mine, theirs)
@@ -217,42 +218,44 @@
         part = x_.at[k, :, :, :, core]
         xc[k] = send(part, part, xc_s.at[k], xc_r.at[k], core_peer)
 
-    def rs_index(q, i, value):
-        done = {(q + 3 - n) % 4 for n in range(i)}
-        now = (q + 3 - i) % 4
-        return tuple(value if d == now else bits[d] if d in done else ALL for d in range(4)), now
+    def rs_dim(q, i):
+        return (q + 3 - i) % 4
+
+    def rs_left(q, i):
+        return [d for d in range(4) if d not in {rs_dim(q, n) for n in range(i)}]
+
+    def split(value, q, i):
+        axis = rs_left(q, i).index(rs_dim(q, i))
+        low, high = (lax.index_in_dim(value, n, axis, keepdims=False) for n in range(2))
+        mine = bits[rs_dim(q, i)] == 0
+        return jnp.where(mine, low, high), jnp.where(mine, high, low)
 
     def rs_send(k, q, i):
-        now = (q + 3 - i) % 4
-        index, _ = rs_index(q, i, 1 - bits[now])
-        rs[k, q, i] = send(p2.at[(k, q) + index], rest[i].at[k, q], rs_s.at[k, q, i], rs_r.at[k, q, i], flips[now])
+        rs[k, q, i] = send(away[i].at[k, q], rest[i].at[k, q], rs_s.at[k, q, i], rs_r.at[k, q, i], flips[rs_dim(q, i)])
+
+    def store(k, q, i, value):
+        stays, goes = split(value, q, i)
+        away[i][k, q] = goes.astype(BF16)
+        rs_send(k, q, i)
+        own[(k, q) + (ALL,) * (3 - i) + (0,) * i] = stays
 
     def second(k):
         xc[k].wait_recv()
         for q in range(Q):
-
-            def tile(a, q=q):
-                acc = None
-                for s in range(2):
-                    lhs = x_[k, s, a].reshape(8 * tokens, half)
-                    rhs = w[pl.ds(q * width, width), s * half : (s + 1) * half]
-                    term = lax.dot_general(lhs, rhs, (((1,), (1,)), ((), ())), preferred_element_type=F32)
-                    acc = term if acc is None else acc + term
-                p2[k, q, a] = acc.astype(BF16).reshape(2, 2, 2, tokens, width)
-
-            pl.loop(0, 2)(tile)
-            rs_send(k, q, 0)
+            acc = None
+            for s in range(2):
+                lhs = x_[k, s].reshape(16 * tokens, half)
+                rhs = w[pl.ds(q * width, width), s * half : (s + 1) * half]
+                term = lax.dot_general(lhs, rhs, (((1,), (1,)), ((), ())), preferred_element_type=F32)
+                acc = term if acc is None else acc + term
+            store(k, q, 0, acc.reshape(2, 2, 2, 2, tokens, width))
 
     def rs_step(k, i):
         for q in range(Q):
-            now = (q + 3 - i) % 4
             rs[k, q, i].wait_recv()
-            index, _ = rs_index(q, i, bits[now])
-            index = (k, q) + index
-            total = p2[index].astype(F32) + rest[i][k, q].astype(F32)
+            total = own[(k, q) + (ALL,) * (3 - i) + (0,) * i] + rest[i][k, q].astype(F32)
             if i < 3:
-                p2[index] = total.astype(BF16)
-                rs_send(k, q, i + 1)
+                store(k, q, i + 1, total)
             else:
                 outv[pl.ds(k * tokens, tokens), pl.ds(q * width, width)] = total.astype(BF16)
 
@@ -263,51 +266,45 @@
             value = lax.dot_general(lhs, rhs, (((0,), (0,)), ((), ())), preferred_element_type=F32)
             grads[0, pl.ds(q * width, width), s * half : (s + 1) * half] = value.astype(BF16)
 
-    for i in range(4):
-        ag_send(0, i)
-    far = [
-        send(resid.at[0, pl.ds(start + k * tokens, tokens), :], far_resid.at[k, b], q_s.at[k, b], q_r.at[k, b], sec_peer)
-        for k in range(K)
-        for b, start in enumerate((start0, start1))
-    ]
-    ag_send(1, 0)
-    ag_done(0)
-    first(0)
-    ag_send(1, 1)
-    ag_send(1, 2)
-    after_core(0)
-    ag_send(1, 3)
-    after_z1(0)
-    after_z2(0)
-    after_swap(0)
-    after_px(0)
-    after_py(0)
-    after_x1(0)
-    ag_done(1)
-    first(1)
-    after_x2(0)
-    after_core(1)
-    second(0)
-    after_z1(1)
-    after_z2(1)
-    after_swap(1)
-    after_px(1)
-    after_py(1)
-    rs_step(0, 0)
-    after_x1(1)
-    rs_step(0, 1)
-    after_x2(1)
-    rs_step(0, 2)
-    second(1)
-    rs_step(0, 3)
-    weight_grads(0)
-    weight_grads(1)
-    rs_step(1, 0)
-    weight_grads(2)
-    rs_step(1, 1)
-    weight_grads(3)
-    rs_step(1, 2)
-    rs_step(1, 3)
+    far = []
+
+    def far_send(k):
+        for b, start in enumerate((start0, start1)):
+            src = resid.at[0, pl.ds(start + k * tokens, tokens), :]
+            far.append(send(src, far_resid.at[k, b], q_s.at[k, b], q_r.at[k, b], sec_peer))
+
+    def stage(k, n):
+        if n < 4:
+            ag_send(k, n)
+        elif n == 4:
+            ag_done(k)
+            first(k)
+        elif n < 12:
+            (after_core, after_z1, after_z2, after_swap, after_sums, after_x1, after_x2)[n - 5](k)
+        elif n == 12:
+            second(k)
+        else:
+            rs_step(k, n - 13)
+
+    far = []
+
+    def far_send(k):
+        for b, start in enumerate((start0, start1)):
+            src = resid.at[0, pl.ds(start + k * tokens, tokens), :]
+            far.append(send(src, far_resid.at[k, b], q_s.at[k, b], q_r.at[k, b], sec_peer))
+
+    at = [0] * K
+    left = list(range(Q))
+    for place, k in enumerate(ORDER):
+        stage(k, at[k])
+        at[k] += 1
+        if place == FAR_AT:
+            for c in range(K):
+                far_send(c)
+        if min(at) >= 13 and left:
+            weight_grads(left.pop(0))
+    for q in left:
+        weight_grads(q)
     final = load(outv, out.at[0], l_o)
     for copy in sends:
         copy.wait_send()
@@ -332,12 +329,14 @@
         vmem((K, 2, tokens, features), BF16),
         vmem((K, 2 * tokens, features), F32),
         vmem((K, 2 * tokens, features), F32),
-        vmem((K, 2 * tokens, 128), F32),
-        vmem((K, 3, 2 * tokens, 128), F32),
-        vmem((K, 2 * tokens, 128), F32),
-        vmem((K, 3, 2 * tokens, 128), F32),
+        vmem((K, 1, 128), F32),
+        vmem((K, 15, 1, 128), F32),
         vmem((K, 2, 2, 2, 2, 2 * tokens, half), BF16),
-        vmem((K, Q) + cube + (tokens, width), BF16),
+        vmem((K, Q, 2, 2, 2, tokens, width), F32),
+        vmem((K, Q, 2, 2, 2, tokens, width), BF16),
+        vmem((K, Q, 2, 2, tokens, width), BF16),
+        vmem((K, Q, 2, tokens, width), BF16),
+        vmem((K, Q, tokens, width), BF16),
         vmem((K, Q, 2, 2, 2, tokens, width), BF16),
         vmem((K, Q, 2, 2, tokens, width), BF16),
         vmem((K, Q, 2, tokens, width), BF16),
@@ -346,7 +345,7 @@
         vmem((1, features), BF16),
         dma, dma((K, Q)), dma((K, 2)), dma, dma,
     ]
-    for shape in ((K, Q, 4), (K, Q, 4), (K,), (K, 2), (K, 2), (K, 2), (K,), (K, 3), (K, 3), (K, 2), (K, 2), (K,)):
+    for shape in ((K, Q, 4), (K, Q, 4), (K,), (K, 2), (K, 2), (K, 2), (K,), (K, 15), (K, 2), (K, 2), (K,)):
         scratch += [dma(shape), dma(shape)]
     hbm = pl.BlockSpec(memory_space=pl.ANY)
     flops = 3 * 2 * rows * 16 * units * features

time: 154 us -> 128 us (0.83); the launches traced: 151 us -> 128 us
  Pallas kernels: 144 us -> 121 us
    pallas_call x1, Pallas kernels: 144 us -> 121 us  [local(): pl.pallas_call(functools.partial(kernel, float(model_width)), out_shape=(...]
where the time goes in v2:
time: 128 us
  Pallas kernels  121 us (95%)
  local copies, waits for them, and re-layouts  6.2 us (5%)
    pallas_call x1, Pallas kernels, local(): pl.pallas_call(functools.partial(kernel, float(model_width)), out_shape=(...  121 us
    unnamed x4, local copies, waits for them, and re-layouts  4.94 us

profile of v2, /device:TPU:1, one launch (start us, length us, event | category | flops | bytes accessed | tf_op | source)
XLA Modules:
  0.0 127.7 jit_solution(5170061904441306816)
XLA Ops:
  0.6 1.3 reshape.7.gain
  1.9 120.8 %shard_map.59 = (bf16[1,3584,512]{2,1,0:T(8,128)(2,1)}, bf16[1,64,3584]{2,1,0:T(8,128)(2,1)}) custom-call(bf16[1,64,3584]{2,1,0:T(8,128)(2,1)} %hidden.1, bf16[1,3584,512]{2,1,0:T(8,128)(2,1)} %weight.1, bf16[1,128,512]{2,1,0:T(8,128)(2,1)} %resid.1, bf16[1,512]{1,0:T(2,128)(2,1)} %reshape.7.gain), custom_call_target="tpu_custom_call" | custom-call | flops 11274289152 | bytes 18350080 | tf_op jit(solution)/shard_map/pallas_call | solution.py:352
  122.7 0.0 copy-start
  122.7 4.2 %copy.8 = bf16[1,3584,512]{2,1,0:T(8,128)(2,1)} copy(bf16[1,3584,512]{2,1,0:T(8,128)(2,1)} %get-tuple-element.4) | data formatting | bytes 7340032
  126.9 0.0 copy-done
  126.9 0.8 copy.9
Async XLA Ops:
  122.7 4.2 %copy-start = (bf16[1,64,3584]{2,1,0:T(8,128)(2,1)S(1)}, bf16[1,64,3584]{2,1,0:T(8,128)(2,1)}, u32[]{:S(2)}) copy-start(bf16[1,64,3584]{2,1,0:T(8,128)(2,1)} %get-tuple-element.5) | copy-start | bytes 1376260

commit v3 on v2

--- a/solution.py
+++ b/solution.py
@@ -15,7 +15,7 @@
 Q = 4
 ALL = slice(None)
 
-ORDER = (0, 1, 2, 3, 0, 2, 1, 3, 0, 1, 3, 0, 2, 1, 0, 2, 3, 0, 1, 0, 1, 2, 2, 0, 3, 1, 3, 0, 1, 2, 0, 3, 1, 2, 0, 3, 1, 2, 0, 3, 1, 0, 2, 3, 1, 2, 1, 3, 2, 0, 2, 3, 3, 1, 2, 3, 1, 2, 0, 3, 2, 0, 1, 3, 0, 2, 1, 3)
+ORDER = (1, 3, 0, 2, 1, 3, 0, 2, 1, 0, 1, 2, 0, 1, 1, 2, 3, 0, 1, 0, 2, 1, 3, 2, 0, 1, 2, 0, 3, 1, 3, 0, 1, 2, 3, 1, 0, 2, 1, 3, 0, 2, 3, 0, 1, 2, 0, 3, 2, 1, 3, 2, 3, 0, 3, 1, 2, 3, 0, 2, 3, 2, 1, 0, 3, 2, 0, 3)
 FAR_AT = 10
 
 
@@ -37,7 +37,7 @@
 
 def kernel(model_width, hidden, weight, resid, gain, grads, out, *scratch):
     (w, h, z, rc, rz1, rz2, own_resid, far_resid, swap_s, swap_r, ps_s, ps_x, x_, own, t0, t1, t2, t3, r0, r1, r2, r3,
-     outv, gv, l_w, l_h, l_r, l_o, l_g,
+     gv, l_w, l_h, l_r, l_g,
      ag_s, ag_r, rs_s, rs_r, zc_s, zc_r, z1_s, z1_r, z2_s, z2_r, q_s, q_r, sw_s, sw_r, px_s, px_r,
      x1_s, x1_r, x2_s, x2_r, xc_s, xc_r) = scratch
     rest = [r0, r1, r2, r3]
@@ -67,7 +67,7 @@
     sec_peer = {"section": 1 - sec}
 
     barrier = pltpu.get_barrier_semaphore()
-    partners = row_peers + [core_peer, z_low, z_high, sec_peer]
+    partners = flips + [core_peer, z_low, z_high, sec_peer]
     for peer in partners:
         pl.semaphore_signal(barrier, inc=1, device_id=peer, device_id_type=MESH)
 
@@ -125,11 +125,17 @@
         for q in range(Q):
             ag[k, q, 3].wait_recv()
 
+    waited = set()
+
+    def once(wait):
+        if wait not in waited:
+            waited.add(wait)
+            wait()
+
     zc, z1, z2, sw, pxs, x1, x2, xc, rs = {}, {}, {}, {}, {}, {}, {}, {}, {}
 
     def first(k):
-        if k == 0:
-            w_load.wait()
+        once(w_load.wait)
 
         acc = None
         for q in range(Q):
@@ -168,13 +174,12 @@
         sw[k] = send(swap_s.at[k], swap_r.at[k], sw_s.at[k], sw_r.at[k], sec_peer)
 
     def after_swap(k):
-        if k == 0:
-            g_load.wait()
+        once(g_load.wait)
         sw[k].wait_recv()
         mine, theirs = swap_s[k], swap_r[k]
         layer = jnp.where(sec == 0, mine, theirs)
         total = jnp.where(sec == 0, theirs, mine)
-        gain_f = gv[...].astype(F32)
+        gain_f = gv[...].astype(F32).reshape(1, 2 * half)
         squares = jnp.sum(layer * layer, axis=1, keepdims=True)
         cross = jnp.sum(total * gain_f * layer, axis=1, keepdims=True)
         line = jnp.where(at_square, squares, 0.0) + jnp.where(at_cross, cross, 0.0)
@@ -184,9 +189,8 @@
     def after_sums(k):
         for copy in pxs[k]:
             copy.wait_recv()
-        if k == 0:
-            for copy in far:
-                copy.wait_recv()
+        for copy in far[k]:
+            copy.wait_recv()
         line = ps_s[k] + jnp.sum(ps_x[k], axis=0)
         squares = jnp.sum(jnp.where(at_square, line, 0.0), axis=1, keepdims=True)
         cross = jnp.sum(jnp.where(at_cross, line, 0.0), axis=1, keepdims=True) / model_width
@@ -195,7 +199,7 @@
         mine, theirs = swap_s[k], swap_r[k]
         layer = jnp.where(sec == 0, mine, theirs)
         total = jnp.where(sec == 0, theirs, mine)
-        gain_f = gv[...].astype(F32)
+        gain_f = gv[...].astype(F32).reshape(1, 2 * half)
         other = far_resid[k].reshape(2 * tokens, 2 * half).astype(F32)
         normed = layer * inv_rms * gain_f
         grad_in = other + inv_rms * gain_f * total - layer * scale
@@ -257,7 +261,7 @@
             if i < 3:
                 store(k, q, i + 1, total)
             else:
-                outv[pl.ds(k * tokens, tokens), pl.ds(q * width, width)] = total.astype(BF16)
+                out[0, pl.ds(k * tokens, tokens), pl.ds(q * width, width)] = total.astype(BF16)
 
     def weight_grads(q):
         lhs = h[q].reshape(K * 16 * tokens, width)
@@ -266,12 +270,13 @@
             value = lax.dot_general(lhs, rhs, (((0,), (0,)), ((), ())), preferred_element_type=F32)
             grads[0, pl.ds(q * width, width), s * half : (s + 1) * half] = value.astype(BF16)
 
-    far = []
+    far = {}
 
     def far_send(k):
+        far[k] = []
         for b, start in enumerate((start0, start1)):
             src = resid.at[0, pl.ds(start + k * tokens, tokens), :]
-            far.append(send(src, far_resid.at[k, b], q_s.at[k, b], q_r.at[k, b], sec_peer))
+            far[k].append(send(src, far_resid.at[k, b], q_s.at[k, b], q_r.at[k, b], sec_peer))
 
     def stage(k, n):
         if n < 4:
@@ -286,12 +291,13 @@
         else:
             rs_step(k, n - 13)
 
-    far = []
+    far = {}
 
     def far_send(k):
+        far[k] = []
         for b, start in enumerate((start0, start1)):
             src = resid.at[0, pl.ds(start + k * tokens, tokens), :]
-            far.append(send(src, far_resid.at[k, b], q_s.at[k, b], q_r.at[k, b], sec_peer))
+            far[k].append(send(src, far_resid.at[k, b], q_s.at[k, b], q_r.at[k, b], sec_peer))
 
     at = [0] * K
     left = list(range(Q))
@@ -305,10 +311,8 @@
             weight_grads(left.pop(0))
     for q in left:
         weight_grads(q)
-    final = load(outv, out.at[0], l_o)
     for copy in sends:
         copy.wait_send()
-    final.wait()
 
 
 def local(section_hidden, section_weight, resid_in, norm_gain):
@@ -341,9 +345,8 @@
         vmem((K, Q, 2, 2, tokens, width), BF16),
         vmem((K, Q, 2, tokens, width), BF16),
         vmem((K, Q, tokens, width), BF16),
-        vmem((rows, units), BF16),
-        vmem((1, features), BF16),
-        dma, dma((K, Q)), dma((K, 2)), dma, dma,
+        vmem((features,), BF16),
+        dma, dma((K, Q)), dma((K, 2)), dma,
     ]
     for shape in ((K, Q, 4), (K, Q, 4), (K,), (K, 2), (K, 2), (K, 2), (K,), (K, 15), (K, 2), (K, 2), (K,)):
         scratch += [dma(shape), dma(shape)]
@@ -352,15 +355,15 @@
     return pl.pallas_call(
         functools.partial(kernel, float(model_width)),
         out_shape=(
-            jax.ShapeDtypeStruct((1, units, features), BF16),
-            jax.ShapeDtypeStruct((1, rows, units), BF16),
+            pltpu.VMEM((1, units, features), BF16),
+            pltpu.VMEM((1, rows, units), BF16),
         ),
         in_specs=[hbm] * 4,
-        out_specs=(pl.BlockSpec(memory_space=pltpu.VMEM), hbm),
+        out_specs=(pl.BlockSpec(memory_space=pltpu.VMEM),) * 2,
         scratch_shapes=scratch,
-        compiler_params=pltpu.CompilerParams(collective_id=0, has_side_effects=True, vmem_limit_bytes=60 * 2**20),
+        compiler_params=pltpu.CompilerParams(collective_id=0, has_side_effects=True, vmem_limit_bytes=59 * 2**20),
         cost_estimate=pl.CostEstimate(flops=flops, bytes_accessed=10 * units * features, transcendentals=0),
-    )(section_hidden, section_weight, resid_in, norm_gain.reshape(1, features))
+    )(section_hidden, section_weight, resid_in, norm_gain)
 
 
 def solution(mesh):

time: 128 us -> 117 us (0.914)
  Pallas kernels: 121 us -> 114 us
  local copies, waits for them, and re-layouts: 6.2 us -> 2.61 us
    pallas_call x1, Pallas kernels: 121 us -> 114 us  [local(): pl.pallas_call(functools.partial(kernel, float(model_width)), out_shape=(...]
    unnamed x4 -> x2, local copies, waits for them, and re-layouts: 4.94 us -> 2.61 us
where the time goes in v3:
time: 117 us
  Pallas kernels  114 us (97%)
  local copies, waits for them, and re-layouts  2.61 us (2%)
    pallas_call x1, Pallas kernels, local(): pl.pallas_call(functools.partial(kernel, float(model_width)), out_shape=(...  114 us
    unnamed x2, local copies, waits for them, and re-layouts  2.61 us

profile of v3, /device:TPU:1, one launch (start us, length us, event | category | flops | bytes accessed | tf_op | source)
XLA Modules:
  0.0 117.2 jit_solution(11838731636073877113)
XLA Ops:
  0.6 114.0 %shard_map.59 = (bf16[1,3584,512]{2,1,0:T(8,128)(2,1)S(1)}, bf16[1,64,3584]{2,1,0:T(8,128)(2,1)S(1)}) custom-call(bf16[1,64,3584]{2,1,0:T(8,128)(2,1)} %hidden.1, bf16[1,3584,512]{2,1,0:T(8,128)(2,1)} %weight.1, bf16[1,128,512]{2,1,0:T(8,128)(2,1)} %resid.1, bf16[512]{0:T(512)(128)(2,1)} %gain.1), custom_call_target="tpu_custom_call" | custom-call | flops 11274289152 | bytes 18350080 | tf_op jit(solution)/shard_map/pallas_call | solution.py:355
  114.6 1.8 %copy.8 = bf16[1,3584,512]{2,1,0:T(8,128)(2,1)} copy(bf16[1,3584,512]{2,1,0:T(8,128)(2,1)S(1)} %get-tuple-element.2) | data formatting | bytes 7340032
  116.5 0.8 copy.9

commit v4 on v3

--- a/solution.py
+++ b/solution.py
@@ -15,8 +15,9 @@
 Q = 4
 ALL = slice(None)
 
-ORDER = (1, 3, 0, 2, 1, 3, 0, 2, 1, 0, 1, 2, 0, 1, 1, 2, 3, 0, 1, 0, 2, 1, 3, 2, 0, 1, 2, 0, 3, 1, 3, 0, 1, 2, 3, 1, 0, 2, 1, 3, 0, 2, 3, 0, 1, 2, 0, 3, 2, 1, 3, 2, 3, 0, 3, 1, 2, 3, 0, 2, 3, 2, 1, 0, 3, 2, 0, 3)
+ORDER = (0, 3, 2, 1, 0, 3, 1, 2, 0, 1, 0, 2, 1, 0, 0, 2, 3, 1, 0, 1, 2, 3, 0, 1, 2, 0, 1, 3, 2, 0, 3, 1, 2, 0, 1, 3, 2, 0, 1, 3, 0, 2, 1, 3, 1, 2, 3, 0, 2, 1, 3, 2, 3, 1, 3, 1, 2, 3, 0, 2, 3, 2, 0, 1, 3, 2, 0, 3)
 FAR_AT = 10
+LAG = 16
 
 
 def mask_of(pos, mask):
@@ -99,6 +100,10 @@
 
     sends = []
 
+    class AllSent:
+        def __init__(self, like, sem):
+            self.wait_send = pltpu.make_async_copy(like, like, sem).wait
+
     def send(src, dst, ssem, rsem, peer):
         copy = pltpu.make_async_remote_copy(src, dst, ssem, rsem, device_id=peer, device_id_type=MESH)
         copy.start()
@@ -132,7 +137,7 @@
             waited.add(wait)
             wait()
 
-    zc, z1, z2, sw, pxs, x1, x2, xc, rs = {}, {}, {}, {}, {}, {}, {}, {}, {}
+    zc, z1, z2, sw, x1, x2, xc, rs = {}, {}, {}, {}, {}, {}, {}, {}
 
     def first(k):
         once(w_load.wait)
@@ -184,11 +189,14 @@
         cross = jnp.sum(total * gain_f * layer, axis=1, keepdims=True)
         line = jnp.where(at_square, squares, 0.0) + jnp.where(at_cross, cross, 0.0)
         ps_s[k] = jnp.sum(line, axis=0, keepdims=True)
-        pxs[k] = [send(ps_s.at[k], ps_x.at[k, n], px_s.at[k, n], px_r.at[k, n], row_peers[n]) for n in range(15)]
+        for n, peer in enumerate(row_peers):
+            pltpu.make_async_remote_copy(
+                ps_s.at[k], ps_x.at[k, n], px_s.at[k], px_r.at[k], device_id=peer, device_id_type=MESH
+            ).start()
+        sends.append(AllSent(ps_x.at[k], px_s.at[k]))
 
     def after_sums(k):
-        for copy in pxs[k]:
-            copy.wait_recv()
+        pltpu.make_async_copy(ps_x.at[k], ps_x.at[k], px_r.at[k]).wait()
         for copy in far[k]:
             copy.wait_recv()
         line = ps_s[k] + jnp.sum(ps_x[k], axis=0)
@@ -270,14 +278,6 @@
             value = lax.dot_general(lhs, rhs, (((0,), (0,)), ((), ())), preferred_element_type=F32)
             grads[0, pl.ds(q * width, width), s * half : (s + 1) * half] = value.astype(BF16)
 
-    far = {}
-
-    def far_send(k):
-        far[k] = []
-        for b, start in enumerate((start0, start1)):
-            src = resid.at[0, pl.ds(start + k * tokens, tokens), :]
-            far[k].append(send(src, far_resid.at[k, b], q_s.at[k, b], q_r.at[k, b], sec_peer))
-
     def stage(k, n):
         if n < 4:
             ag_send(k, n)
@@ -301,6 +301,7 @@
 
     at = [0] * K
     left = list(range(Q))
+    sent, ended = [], 0
     for place, k in enumerate(ORDER):
         stage(k, at[k])
         at[k] += 1
@@ -309,9 +310,14 @@
                 far_send(c)
         if min(at) >= 13 and left:
             weight_grads(left.pop(0))
+        sent.append(len(sends))
+        if place >= LAG:
+            while ended < sent[place - LAG]:
+                sends[ended].wait_send()
+                ended += 1
     for q in left:
         weight_grads(q)
-    for copy in sends:
+    for copy in sends[ended:]:
         copy.wait_send()
 
 
@@ -348,7 +354,7 @@
         vmem((features,), BF16),
         dma, dma((K, Q)), dma((K, 2)), dma,
     ]
-    for shape in ((K, Q, 4), (K, Q, 4), (K,), (K, 2), (K, 2), (K, 2), (K,), (K, 15), (K, 2), (K, 2), (K,)):
+    for shape in ((K, Q, 4), (K, Q, 4), (K,), (K, 2), (K, 2), (K, 2), (K,), (K,), (K, 2), (K, 2), (K,)):
         scratch += [dma(shape), dma(shape)]
     hbm = pl.BlockSpec(memory_space=pl.ANY)
     flops = 3 * 2 * rows * 16 * units * features

time: 117 us -> 115 us (0.983)
  Pallas kernels: 114 us -> 111 us
    pallas_call x1, Pallas kernels: 114 us -> 111 us  [local(): pl.pallas_call(functools.partial(kernel, float(model_width)), out_shape=(...]
where the time goes in v4:
time: 115 us
  Pallas kernels  111 us (97%)
  local copies, waits for them, and re-layouts  2.61 us (2%)
    pallas_call x1, Pallas kernels, local(): pl.pallas_call(functools.partial(kernel, float(model_width)), out_shape=(...  111 us
    unnamed x2, local copies, waits for them, and re-layouts  2.61 us

profile of v4, /device:TPU:1, one launch (start us, length us, event | category | flops | bytes accessed | tf_op | source)
XLA Modules:
  0.0 114.7 jit_solution(16816024829856416010)
XLA Ops:
  0.6 111.5 %shard_map.59 = (bf16[1,3584,512]{2,1,0:T(8,128)(2,1)S(1)}, bf16[1,64,3584]{2,1,0:T(8,128)(2,1)S(1)}) custom-call(bf16[1,64,3584]{2,1,0:T(8,128)(2,1)} %hidden.1, bf16[1,3584,512]{2,1,0:T(8,128)(2,1)} %weight.1, bf16[1,128,512]{2,1,0:T(8,128)(2,1)} %resid.1, bf16[512]{0:T(512)(128)(2,1)} %gain.1), custom_call_target="tpu_custom_call" | custom-call | flops 11274289152 | bytes 18350080 | tf_op jit(solution)/shard_map/pallas_call | solution.py:361
  112.1 1.8 %copy.8 = bf16[1,3584,512]{2,1,0:T(8,128)(2,1)} copy(bf16[1,3584,512]{2,1,0:T(8,128)(2,1)S(1)} %get-tuple-element.2) | data formatting | bytes 7340032
  113.9 0.8 copy.9

commit v5 on v4

--- a/solution.py
+++ b/solution.py
@@ -15,7 +15,7 @@
 Q = 4
 ALL = slice(None)
 
-ORDER = (0, 3, 2, 1, 0, 3, 1, 2, 0, 1, 0, 2, 1, 0, 0, 2, 3, 1, 0, 1, 2, 3, 0, 1, 2, 0, 1, 3, 2, 0, 3, 1, 2, 0, 1, 3, 2, 0, 1, 3, 0, 2, 1, 3, 1, 2, 3, 0, 2, 1, 3, 2, 3, 1, 3, 1, 2, 3, 0, 2, 3, 2, 0, 1, 3, 2, 0, 3)
+ORDER = (2, 1, 0, 2, 3, 1, 0, 2, 1, 0, 2, 1, 2, 3, 0, 2, 1, 3, 1, 2, 0, 3, 1, 2, 0, 1, 2, 3, 0, 3, 1, 2, 0, 1, 3, 2, 0, 1, 3, 2, 0, 2, 3, 1, 0, 1, 3, 0, 2, 3, 0, 3, 1, 3, 0, 1, 3, 0, 2, 3, 1, 0, 2, 3, 0, 2, 1, 3)
 FAR_AT = 10
 LAG = 16
 

time: 115 us -> 118 us (1.026)
  Pallas kernels: 111 us -> 114 us
    pallas_call x1, Pallas kernels: 111 us -> 114 us  [local(): pl.pallas_call(functools.partial(kernel, float(model_width)), out_shape=(...]
where the time goes in v5:
time: 118 us; the launch traced here: 117 us
  Pallas kernels  114 us (97%)
  local copies, waits for them, and re-layouts  2.61 us (2%)
    pallas_call x1, Pallas kernels, local(): pl.pallas_call(functools.partial(kernel, float(model_width)), out_shape=(...  114 us
    unnamed x2, local copies, waits for them, and re-layouts  2.61 us

profile of v5, /device:TPU:1, one launch (start us, length us, event | category | flops | bytes accessed | tf_op | source)
XLA Modules:
  0.0 116.8 jit_solution(11073444027061075018)
XLA Ops:
  0.6 113.6 %shard_map.59 = (bf16[1,3584,512]{2,1,0:T(8,128)(2,1)S(1)}, bf16[1,64,3584]{2,1,0:T(8,128)(2,1)S(1)}) custom-call(bf16[1,64,3584]{2,1,0:T(8,128)(2,1)} %hidden.1, bf16[1,3584,512]{2,1,0:T(8,128)(2,1)} %weight.1, bf16[1,128,512]{2,1,0:T(8,128)(2,1)} %resid.1, bf16[512]{0:T(512)(128)(2,1)} %gain.1), custom_call_target="tpu_custom_call" | custom-call | flops 11274289152 | bytes 18350080 | tf_op jit(solution)/shard_map/pallas_call | solution.py:361
  114.2 1.8 %copy.8 = bf16[1,3584,512]{2,1,0:T(8,128)(2,1)} copy(bf16[1,3584,512]{2,1,0:T(8,128)(2,1)S(1)} %get-tuple-element.2) | data formatting | bytes 7340032
  116.0 0.8 copy.9
